TPU v7x, 512 devices: a whole 4x8x8 slice. The times are simulated.
512 devices in a mesh: grp: 16 (over z, core), aux: 32 (over x, y).
Axes of the slice: x: 4, y: 8, z: 8, core: 2. Of those that a mesh axis runs over, the one named last changes fastest.
Arguments:
- integrals: bfloat16 [2048, 262144], P('aux', 'grp'), parts along dimension 1, may hold values from -6 to 6
- inverses: bfloat16 [4, 512, 512], P(None, 'aux'), as said below
- lower_blocks: bfloat16 [6, 512, 512], P(None, 'aux'), may hold values from -0.25 to 0.25
Outputs:
- solved: bfloat16 [2048, 262144], P(None, ('grp', 'aux')), parts along dimension 1
There are 16 independent parts, one for each index of `grp`. A program takes and returns all parts, laid end to end along the dimension named above; an argument that names none is the same for every part. Nothing has to cross between parts.
Inputs may be any that keep to these rules, and one draw needn't show every extreme that they name: Each inverses[k] is lower triangular with diagonal entries between 0.5 and 1.5.
All inputs are finite; a program needn't handle non-finite values.
Results may differ from a plain program's by a relative error of at most 0.007.
Values may be sent and summed in bfloat16 or wider, within the bound.
No kernel may reach another device: no remote copies, remote signals or barrier semaphores. Data moves between devices by JAX's collectives and lax.ppermute only.
A program may use at most 64 MiB of HBM per device.

v0:
```python
import jax
import jax.numpy as jnp
from jax import lax
from jax.sharding import PartitionSpec as P


def local(integrals, inverses, lower_blocks):
    inv_all, low_all = (
        lax.all_gather(inverses, "aux", axis=1, tiled=True),
        lax.all_gather(lower_blocks, "aux", axis=1, tiled=True),
    )
    count = inv_all.shape[0]
    panel = inv_all.shape[1]
    width = integrals.shape[0]
    groups = lax.axis_size("aux")
    rows = integrals.shape[1] // groups
    sectioned = integrals.reshape(width, groups, rows)
    block = lax.all_to_all(sectioned, "aux", split_axis=1, concat_axis=0, tiled=True)
    columns = block.reshape(block.shape[0], block.shape[2])
    outs = []
    for k in range(count):
        acc = columns[k * panel : (k + 1) * panel].astype(jnp.float32)
        for j in range(k):
            acc = acc - jnp.dot(
                low_all[k * (k - 1) // 2 + j], outs[j], preferred_element_type=jnp.float32
            )
        rest = acc.astype(jnp.bfloat16)
        outs.append(
            jnp.dot(inv_all[k], rest, preferred_element_type=jnp.float32).astype(jnp.bfloat16)
        )
    return jnp.concatenate(outs, axis=0)


def solution(mesh):
    placed = (P("aux", "grp"), P(None, "aux", None), P(None, "aux", None))
    return jax.shard_map(
        local, mesh=mesh, in_specs=placed, out_specs=P(None, ("grp", "aux")), check_vma=False
    )
```

profile of v0, /device:TPU:64, one launch (start us, length us, event | category | flops | bytes accessed | tf_op | source)
XLA Modules:
  0.0 209.6 jit_solution(11446586706947685064)
XLA Ops:
  6.5 0.0 all-gather.3.cloned.1.call-start
  6.5 0.7 all-gather.3.cloned.1.call-update
  7.3 0.0 all-gather.5.cloned.1.call-start
  7.3 0.7 all-gather.5.cloned.1.call-update
  8.0 1.9 copy.17
  9.9 63.3 %all_to_all.15 = bf16[64,32,512]{2,0,1:T(8,128)(2,1)S(1)} all-to-all(bf16[64,32,512]{2,0,1:T(8,128)(2,1)S(1)} %bitcast.100), channel_id=1, replica_groups=mesh['grp'=16,'aux'=32] {'aux'}, dimensions={1} | all-to-all | bytes 4194304 | tf_op jit(solution)/shard_map/all_to_all | solution.py:18
  73.2 0.1 fusion.10
  73.3 0.2 bitcast_convert_fusion.2
  73.5 1.4 copy.12
  74.8 1.3 bitcast_convert_fusion
  76.2 0.3 copy.13
  76.5 1.6 copy.14
  78.1 24.0 %all-gather.3.cloned.1.call-done = bf16[4,512,512]{2,1,0:T(8,128)(2,1)} async-done(((bf16[4,16,512]{2,1,0:T(8,128)(2,1)}), bf16[4,512,512]{2,1,0:T(8,128)(2,1)}) %all-gather.3.cloned.1.call-update) | async-done | bytes 2097168 | tf_op jit(solution)/shard_map/all_gather | solution.py:9
  102.1 1.5 convolution_convert_fusion.3
  103.6 84.3 %all-gather.5.cloned.1.call-done = bf16[6,512,512]{2,1,0:T(8,128)(2,1)} async-done(((bf16[6,16,512]{2,1,0:T(8,128)(2,1)}), bf16[6,512,512]{2,1,0:T(8,128)(2,1)}) %all-gather.5.cloned.1.call-update) | async-done | bytes 3145744 | tf_op jit(solution)/shard_map/all_gather | solution.py:10
  187.9 2.4 %convolution_convert_fusion.2 = bf16[512,512]{0,1:T(8,128)(2,1)S(1)} fusion(f32[512,512]{0,1:T(8,128)} %copy.12, bf16[512,512]{1,0:T(8,128)(2,1)S(1)} %convolution_convert_fusion.3, bf16[4,512,512]{2,1,0:T(8,128)(2,1)} %all-gather.3.cloned.1.call-done, bf16[6,512,512]{2,1,0:T(8,128)(2,1)} %all-gather.5.cloned.1.call-done), kind=kOutput, calls=%fused_computation.16 | convolution fusion | flops 537657344 | bytes 3145728 | tf_op jit(solution)/shard_map/dot_general | solution.py:29
  190.3 2.5 %fusion.4 = f32[512,512]{0,1:T(8,128)} fusion(f32[512,512]{0,1:T(8,128)S(1)} %copy.13, bf16[512,512]{1,0:T(8,128)(2,1)S(1)} %convolution_convert_fusion.3, bf16[6,512,512]{2,1,0:T(8,128)(2,1)} %all-gather.5.cloned.1.call-done), kind=kOutput, calls=%fused_computation.11 | convolution fusion | flops 268697600 | bytes 3145728 | tf_op jit(solution)/shard_map/dot_general | solution.py:24
  192.8 1.5 fusion.2
  194.3 3.2 %convolution_convert_fusion.1 = bf16[512,512]{0,1:T(8,128)(2,1)} fusion(f32[512,512]{0,1:T(8,128)} %fusion.4, bf16[512,512]{0,1:T(8,128)(2,1)S(1)} %convolution_convert_fusion.2, bf16[4,512,512]{2,1,0:T(8,128)(2,1)} %all-gather.3.cloned.1.call-done, bf16[6,512,512]{2,1,0:T(8,128)(2,1)} %all-gather.5.cloned.1.call-done), kind=kOutput, calls=%fused_computation.15 | convolution fusion | flops 537657344 | bytes 3145728 | tf_op jit(solution)/shard_map/dot_general | solution.py:29
  197.5 1.5 fusion.1
  199.0 0.0 copy-start
  199.0 2.3 %fusion.9 = bf16[512,512]{1,0:T(8,128)(2,1)S(1)} fusion(f32[512,512]{0,1:T(8,128)S(1)} %fusion.1, bf16[512,512]{0,1:T(8,128)(2,1)} %convolution_convert_fusion.1, bf16[4,512,512]{2,1,0:T(8,128)(2,1)} %all-gather.3.cloned.1.call-done, bf16[6,512,512]{2,1,0:T(8,128)(2,1)} %all-gather.5.cloned.1.call-done), kind=kOutput, calls=%fused_computation.21 | convolution fusion | flops 537657344 | bytes 3145728 | tf_op jit(solution)/shard_map/dot_general | solution.py:29
  201.3 0.0 copy-done
  201.3 1.5 pad_maximum_fusion
Async XLA Ops:
  6.5 95.6 %all-gather.3.cloned.1.call-start = ((), (), s32[]{:S(2)}) async-start(), calls=%async_computation.1 | async-start | bytes 2162688 | tf_op jit(solution)/shard_map/all_gather | solution.py:9
  7.3 180.6 %all-gather.5.cloned.1.call-start = ((), (), s32[]{:S(2)}) async-start(), calls=%async_computation.2 | async-start | bytes 3244032 | tf_op jit(solution)/shard_map/all_gather | solution.py:10
  199.0 2.3 %copy-start = (bf16[512,512]{0,1:T(8,128)(2,1)S(1)}, bf16[512,512]{0,1:T(8,128)(2,1)}, u32[]{:S(2)}) copy-start(bf16[512,512]{0,1:T(8,128)(2,1)} %convolution_convert_fusion.1) | copy-start | bytes 1572868
Sparse Core Ops, SparseCore 0:
  10.5 91.5 all-gather.2
  105.3 82.5 all-gather.4
where the time goes:
time: 210 us
  waiting for transfers between devices  110 us (52%)
  blocking collectives  63.3 us (30%)
  matrix products  14.8 us (7%)
  between operations  13.5 us (6%)
  local copies, waits for them, and re-layouts  5.24 us (2%)
  other arithmetic  2.94 us (1%)
    all_gather x1, waiting for transfers between devices, local(): lax.all_gather(lower_blocks, 'aux', axis=1, tiled=True)  84.3 us
    all_to_all x1, blocking collectives, local(): lax.all_to_all(sectioned, 'aux', split_axis=1, concat_axis=0, tiled=True)  63.3 us
    all_gather x1, waiting for transfers between devices, local(): lax.all_gather(inverses, 'aux', axis=1, tiled=True)  24 us
    dot_general x4, matrix products, local(): jnp.dot(inv_all[k], rest, preferred_element_type=jnp.float32)  9.29 us
    dot_general x3, matrix products, local(): jnp.dot(low_all[k * (k - 1) // 2 + j], outs[j], preferred_element_type=jn...  5.55 us
  transfers between devices with their start and end apart: 2, of which 2 were waited for; matrix products, arithmetic and copies ran while one was open for 4% of the time, Pallas kernels for 0%

commit v1 on v0

--- a/solution.py
+++ b/solution.py
@@ -4,9 +4,14 @@
 from jax.sharding import PartitionSpec as P
 
 
+def gather_over(block, axis, dim):
+    repeated = jnp.stack([block] * lax.axis_size(axis))
+    return jnp.concatenate(lax.all_to_all(repeated, axis, 0, 0), axis=dim)
+
+
 def local(integrals, inverses, lower_blocks):
     inv_all, low_all = (
-        lax.all_gather(inverses, "aux", axis=1, tiled=True),
+        gather_over(inverses, "aux", 1),
         lax.all_gather(lower_blocks, "aux", axis=1, tiled=True),
     )
     count = inv_all.shape[0]

time: 210 us -> 173 us (0.82)
  the two profiles are of different devices: /device:TPU:64 before, /device:TPU:256 now
where the time goes in v1:
time: 173 us; the launch traced here: 172 us
  waiting for transfers between devices  109 us (63%)
  starting transfers between devices  15.4 us (9%)
  matrix products  15 us (9%)
  local copies, waits for them, and re-layouts  14.7 us (8%)
  between operations  13.5 us (8%)
  other arithmetic  4.41 us (3%)
    all_to_all x1, waiting for transfers between devices, gather_over(): return jnp.concatenate(lax.all_to_all(repeated, axis, 0, 0), axis=dim)  54.9 us
    all_to_all x1, waiting for transfers between devices, local(): lax.all_to_all(sectioned, 'aux', split_axis=1, concat_axis=0, tiled=True)  53.8 us
    all_to_all x1, starting transfers between devices, local(): lax.all_to_all(sectioned, 'aux', split_axis=1, concat_axis=0, tiled=True)  10.1 us
    dot_general x4, matrix products, local(): jnp.dot(inv_all[k], rest, preferred_element_type=jnp.float32)  8.08 us
    dot_general x3, matrix products, local(): jnp.dot(low_all[k * (k - 1) // 2 + j], outs[j], preferred_element_type=jn...  6.91 us
    convert_element_type x3, local copies, waits for them, and re-layouts, local(): acc = columns[k * panel:(k + 1) * panel].astype(jnp.float32)  5.43 us
    all_to_all x1, starting transfers between devices, gather_over(): return jnp.concatenate(lax.all_to_all(repeated, axis, 0, 0), axis=dim)  5.29 us
  transfers between devices with their start and end apart: 3, of which 2 were waited for; matrix products, arithmetic and copies ran while one was open for 8% of the time, Pallas kernels for 0%

profile of v1, /device:TPU:256, one launch (start us, length us, event | category | flops | bytes accessed | tf_op | source)
XLA Modules:
  0.0 172.4 jit_solution(17540865308857866971)
XLA Ops:
  6.5 3.2 %copy.17 = bf16[8,32,8,512]{3,2,0,1:T(8,128)(2,1)} copy(bf16[8,32,8,512]{3,2,1,0:T(8,128)(2,1)} %bitcast.99) | data formatting | bytes 4194304 | tf_op jit(solution)/shard_map/reshape | solution.py:22
  9.7 0.0 copy-start.5
  9.7 10.1 %all-to-all-start.1 = ((bf16[64,32,512]{2,0,1:T(8,128)(2,1)}), bf16[64,32,512]{2,0,1:T(8,128)(2,1)S(1)}, u32[]{:S(2)}, u32[]{:S(2)}) async-start(bf16[64,32,512]{2,0,1:T(8,128)(2,1)} %bitcast.98), calls=%async_computation.1 | async-start | bytes 4194304 | tf_op jit(solution)/shard_map/all_to_all | solution.py:23
  19.8 0.0 all-gather.2.cloned.1.call-start
  19.9 0.7 all-gather.2.cloned.1.call-update
  20.6 53.8 %all-to-all-done.1 = bf16[64,32,512]{2,0,1:T(8,128)(2,1)S(1)} async-done(((bf16[64,32,512]{2,0,1:T(8,128)(2,1)}), bf16[64,32,512]{2,0,1:T(8,128)(2,1)S(1)}, u32[]{:S(2)}, u32[]{:S(2)}) %all-to-all-start.1) | async-done | bytes 2097184 | tf_op jit(solution)/shard_map/all_to_all | solution.py:23
  74.4 0.0 copy-done.5
  74.4 0.0 copy-start
  74.4 1.8 %stack.2 = bf16[32,4,16,512]{3,2,1,0:T(8,128)(2,1)} broadcast(bf16[4,16,512]{2,1,0:T(8,128)(2,1)S(1)} %copy-done.5), dimensions={1,2,3} | broadcast | bytes 2162688 | tf_op jit(solution)/shard_map/stack | solution.py:8
  76.2 0.3 copy-done
  76.4 5.3 %all-to-all-start = ((bf16[32,4,16,512]{3,2,1,0:T(8,128)(2,1)}), bf16[32,4,16,512]{3,2,1,0:T(8,128)(2,1)S(1)}, u32[]{:S(2)}, u32[]{:S(2)}) async-start(bf16[32,4,16,512]{3,2,1,0:T(8,128)(2,1)} %stack.2), calls=%async_computation | async-start | bytes 4194304 | tf_op jit(solution)/shard_map/all_to_all | solution.py:9
  81.7 2.7 %fusion.10 = (bf16[8,64,1,512]{3,1,0,2:T(8,128)(2,1)}, bf16[8,64,1,512]{3,1,0,2:T(8,128)(2,1)}, bf16[8,64,1,512]{3,1,0,2:T(8,128)(2,1)S(1)}, bf16[8,64,1,512]{3,1,0,2:T(8,128)(2,1)}) fusion(bf16[32,64,1,512]{3,1,0,2:T(8,128)(2,1)} %bitcast.97), kind=kLoop, calls=%fused_computation.31 | loop fusion | bytes 4194304 | tf_op jit(solution)/shard_map/slice | solution.py:27
  84.4 0.2 bitcast_convert_fusion.2
  84.6 1.3 copy.12
  85.9 2.8 %bitcast_convert_fusion = (f32[512,512]{1,0:T(8,128)}, f32[512,512]{1,0:T(8,128)}) fusion(bf16[8,64,1,512]{3,1,0,2:T(8,128)(2,1)} %get-tuple-element.6, bf16[8,64,1,512]{3,1,0,2:T(8,128)(2,1)} %get-tuple-element.5), kind=kLoop, calls=%fused_computation.28 | loop fusion | flops 524288 | bytes 3145728 | tf_op jit(solution)/shard_map/convert_element_type | solution.py:27
  88.7 1.6 copy.13
  90.3 2.5 %copy.14 = f32[512,512]{0,1:T(8,128)} copy(f32[512,512]{1,0:T(8,128)} %get-tuple-element.13) | data formatting | bytes 2097152 | tf_op jit(solution)/shard_map/convert_element_type | solution.py:27
  92.8 54.9 %all-to-all-done = bf16[32,4,16,512]{3,2,1,0:T(8,128)(2,1)S(1)} async-done(((bf16[32,4,16,512]{3,2,1,0:T(8,128)(2,1)}), bf16[32,4,16,512]{3,2,1,0:T(8,128)(2,1)S(1)}, u32[]{:S(2)}, u32[]{:S(2)}) %all-to-all-start) | async-done | bytes 2097184 | tf_op jit(solution)/shard_map/all_to_all | solution.py:9
  147.8 0.0 copy-start.1
  147.8 1.2 fusion.11
  149.0 0.1 copy-done.1
  149.1 0.4 convolution_convert_fusion.3
  149.5 0.0 all-gather.2.cloned.1.call-done
  149.5 2.5 %fusion.4 = f32[512,512]{0,1:T(8,128)} fusion(f32[512,512]{0,1:T(8,128)S(1)} %copy.13, bf16[512,512]{1,0:T(8,128)(2,1)S(1)} %convolution_convert_fusion.3, bf16[6,512,512]{2,1,0:T(8,128)(2,1)} %all-gather.2.cloned.1.call-done), kind=kOutput, calls=%fused_computation.11 | convolution fusion | flops 268697600 | bytes 3145728 | tf_op jit(solution)/shard_map/dot_general | solution.py:29
  152.1 1.9 %fusion.2 = f32[512,512]{0,1:T(8,128)S(1)} fusion(f32[512,512]{0,1:T(8,128)} %copy.14, bf16[512,512]{1,0:T(8,128)(2,1)S(1)} %convolution_convert_fusion.3, bf16[6,512,512]{2,1,0:T(8,128)(2,1)} %all-gather.2.cloned.1.call-done), kind=kOutput, calls=%fused_computation.7 | convolution fusion | flops 268697600 | bytes 3145728 | tf_op jit(solution)/shard_map/dot_general | solution.py:29
  153.9 0.0 copy-start.2
  154.0 2.4 %convolution_convert_fusion.2 = bf16[512,512]{0,1:T(8,128)(2,1)S(1)} fusion(bf16[512,512]{1,0:T(8,128)(2,1)} %bitcast.105, f32[512,512]{0,1:T(8,128)} %copy.12, bf16[512,512]{1,0:T(8,128)(2,1)S(1)} %convolution_convert_fusion.3, bf16[6,512,512]{2,1,0:T(8,128)(2,1)} %all-gather.2.cloned.1.call-done), kind=kOutput, calls=%fused_computation.16 | convolution fusion | flops 537657344 | bytes 3145728 | tf_op jit(solution)/shard_map/dot_general | solution.py:34
  156.4 2.5 %fusion.1 = f32[512,512]{0,1:T(8,128)} fusion(f32[512,512]{0,1:T(8,128)S(1)} %fusion.2, bf16[512,512]{0,1:T(8,128)(2,1)S(1)} %convolution_convert_fusion.2, bf16[6,512,512]{2,1,0:T(8,128)(2,1)} %all-gather.2.cloned.1.call-done), kind=kOutput, calls=%fused_computation.5 | convolution fusion | flops 268697600 | bytes 3145728 | tf_op jit(solution)/shard_map/dot_general | solution.py:29
  158.9 0.0 copy-start.3
  158.9 0.0 copy-done.2
  158.9 2.9 %convolution_convert_fusion.1 = bf16[512,512]{0,1:T(8,128)(2,1)} fusion(bf16[512,512]{1,0:T(8,128)(2,1)} %bitcast.104, f32[512,512]{0,1:T(8,128)S(1)} %copy-done.2, bf16[512,512]{0,1:T(8,128)(2,1)S(1)} %convolution_convert_fusion.2, bf16[6,512,512]{2,1,0:T(8,128)(2,1)} %all-gather.2.cloned.1.call-done), kind=kOutput, calls=%fused_computation.15 | convolution fusion | flops 537657344 | bytes 3145728 | tf_op jit(solution)/shard_map/dot_general | solution.py:34
  161.9 0.0 copy-start.4
  161.9 0.0 copy-done.3
  161.9 2.3 %fusion.9 = bf16[512,512]{1,0:T(8,128)(2,1)S(1)} fusion(bf16[512,512]{1,0:T(8,128)(2,1)} %bitcast.103, f32[512,512]{0,1:T(8,128)S(1)} %copy-done.3, bf16[512,512]{0,1:T(8,128)(2,1)} %convolution_convert_fusion.1, bf16[6,512,512]{2,1,0:T(8,128)(2,1)} %all-gather.2.cloned.1.call-done), kind=kOutput, calls=%fused_computation.21 | convolution fusion | flops 537657344 | bytes 3145728 | tf_op jit(solution)/shard_map/dot_general | solution.py:34
  164.1 0.0 copy-done.4
  164.1 1.5 pad_maximum_fusion
Async XLA Ops:
  9.7 64.7 %copy-start.5 = (bf16[4,16,512]{2,1,0:T(8,128)(2,1)S(1)}, bf16[4,16,512]{2,1,0:T(8,128)(2,1)}, u32[]{:S(2)}) copy-start(bf16[4,16,512]{2,1,0:T(8,128)(2,1)} %param.4) | copy-start | bytes 196612
  9.7 64.7 %all-to-all-start.1 = ((bf16[64,32,512]{2,0,1:T(8,128)(2,1)}), bf16[64,32,512]{2,0,1:T(8,128)(2,1)S(1)}, u32[]{:S(2)}, u32[]{:S(2)}) async-start(bf16[64,32,512]{2,0,1:T(8,128)(2,1)} %bitcast.98), calls=%async_computation.1 | async-start | bytes 4194304 | tf_op jit(solution)/shard_map/all_to_all | solution.py:23
  19.8 129.7 %all-gather.2.cloned.1.call-start = ((), (), s32[]{:S(2)}) async-start(), calls=%async_computation.2 | async-start | bytes 3244032 | tf_op jit(solution)/shard_map/all_gather | solution.py:15
  74.4 2.0 %copy-start = (bf16[64,32,512]{2,0,1:T(8,128)(2,1)}, bf16[64,32,512]{2,0,1:T(8,128)(2,1)S(1)}, u32[]{:S(2)}) copy-start(bf16[64,32,512]{2,0,1:T(8,128)(2,1)S(1)} %all-to-all-done.1) | copy-start | bytes 6291460
  76.4 71.4 %all-to-all-start = ((bf16[32,4,16,512]{3,2,1,0:T(8,128)(2,1)}), bf16[32,4,16,512]{3,2,1,0:T(8,128)(2,1)S(1)}, u32[]{:S(2)}, u32[]{:S(2)}) async-start(bf16[32,4,16,512]{3,2,1,0:T(8,128)(2,1)} %stack.2), calls=%async_computation | async-start | bytes 4194304 | tf_op jit(solution)/shard_map/all_to_all | solution.py:9
  147.8 1.3 copy-start.1
  153.9 5.0 %copy-start.2 = (f32[512,512]{0,1:T(8,128)S(1)}, f32[512,512]{0,1:T(8,128)}, u32[]{:S(2)}) copy-start(f32[512,512]{0,1:T(8,128)} %fusion.4) | copy-start | bytes 3145732
  158.9 2.9 %copy-start.3 = (f32[512,512]{0,1:T(8,128)S(1)}, f32[512,512]{0,1:T(8,128)}, u32[]{:S(2)}) copy-start(f32[512,512]{0,1:T(8,128)} %fusion.1) | copy-start | bytes 3145732
  161.9 2.3 %copy-start.4 = (bf16[512,512]{0,1:T(8,128)(2,1)S(1)}, bf16[512,512]{0,1:T(8,128)(2,1)}, u32[]{:S(2)}) copy-start(bf16[512,512]{0,1:T(8,128)(2,1)} %convolution_convert_fusion.1) | copy-start | bytes 1572868
Sparse Core Ops, SparseCore 0:
  23.8 120.5 all-gather.1

commit v2 on v0

--- a/solution.py
+++ b/solution.py
@@ -5,6 +5,15 @@
 
 
 def local(integrals, inverses, lower_blocks):
+
+    def produce_the_map(raw):
+        t_next = lax.axis_size("aux")
+        z = jnp.split(raw, t_next, 1)
+        tmp = jnp.stack(z, 0)
+        b_now = lax.all_to_all(tmp, "aux", 0, 0)
+        lower = jnp.concatenate(b_now, axis=0)
+        return lower
+
     inv_all, low_all = (
         lax.all_gather(inverses, "aux", axis=1, tiled=True),
         lax.all_gather(lower_blocks, "aux", axis=1, tiled=True),
@@ -15,7 +24,7 @@
     groups = lax.axis_size("aux")
     rows = integrals.shape[1] // groups
     sectioned = integrals.reshape(width, groups, rows)
-    block = lax.all_to_all(sectioned, "aux", split_axis=1, concat_axis=0, tiled=True)
+    block = produce_the_map(sectioned)
     columns = block.reshape(block.shape[0], block.shape[2])
     outs = []
     for k in range(count):

time: 210 us -> 211 us (level)
  local copies, waits for them, and re-layouts: 5.24 us -> 11.5 us
  waiting for transfers between devices: 110 us -> 104 us
    all_gather x1, waiting for transfers between devices: 24 us -> 17.1 us  [local(): lax.all_gather(inverses, 'aux', axis=1, tiled=True)]
    split x0 -> x2, local copies, waits for them, and re-layouts: none -> 4.54 us  [produce_the_map(): z = jnp.split(raw, t_next, 1)]
    unnamed x2 -> x36, local copies, waits for them, and re-layouts: 0.01 us -> 2.77 us
  transfers between devices with their start and end apart: 2 -> 2, of which waited for: 2 -> 2; matrix products, arithmetic and copies ran while one was open for 4% -> 7% of each run, Pallas kernels for 0% -> 0%
where the time goes in v2:
time: 211 us; the launch traced here: 210 us
  waiting for transfers between devices  104 us (49%)
  blocking collectives  63.3 us (30%)
  matrix products  14.8 us (7%)
  between operations  13.8 us (7%)
  local copies, waits for them, and re-layouts  11.5 us (5%)
  other arithmetic  2.94 us (1%)
    all_gather x1, waiting for transfers between devices, local(): lax.all_gather(lower_blocks, 'aux', axis=1, tiled=True)  85.1 us
    all_to_all x1, blocking collectives, produce_the_map(): b_now = lax.all_to_all(tmp, 'aux', 0, 0)  63.3 us
    all_gather x1, waiting for transfers between devices, local(): lax.all_gather(inverses, 'aux', axis=1, tiled=True)  17.1 us
    dot_general x4, matrix products, local(): jnp.dot(inv_all[k], rest, preferred_element_type=jnp.float32)  9.29 us
    dot_general x3, matrix products, local(): jnp.dot(low_all[k * (k - 1) // 2 + j], outs[j], preferred_element_type=jn...  5.55 us
    split x2, local copies, waits for them, and re-layouts, produce_the_map(): z = jnp.split(raw, t_next, 1)  4.54 us
  transfers between devices with their start and end apart: 2, of which 2 were waited for; matrix products, arithmetic and copies ran while one was open for 7% of the time, Pallas kernels for 0%

profile of v2, /device:TPU:64, one launch (start us, length us, event | category | flops | bytes accessed | tf_op | source)
XLA Modules:
  0.0 210.0 jit_solution(5672783405979722442)
XLA Ops:
  6.5 0.0 all-gather.3.cloned.1.call-start
  6.5 0.7 all-gather.3.cloned.1.call-update
  7.3 0.0 all-gather.5.cloned.1.call-start
  7.3 0.7 all-gather.5.cloned.1.call-update
  8.0 2.4 %copy.621 = bf16[8,8,32,512]{3,2,1,0:T(8,128)(2,1)S(1)} copy(bf16[8,8,32,512]{3,1,2,0:T(8,128)(2,1)} %bitcast.162) | data formatting | bytes 4194304
  10.4 1.7 fusion.12
  12.1 2.8 %fusion.11 = (bf16[64,1,512]{2,1,0:T(2,128)(2,1)S(1)}, bf16[64,1,512]{2,1,0:T(2,128)(2,1)S(1)}, bf16[64,1,512]{2,1,0:T(2,128)(2,1)S(1)}, bf16[64,1,512]{2,1,0:T(...) fusion(bf16[64,32,512]{2,1,0:T(8,128)(2,1)S(1)} %bitcast.160), kind=kLoop, calls=%fused_computation.67 | loop fusion | bytes 2490368 | tf_op jit(solution)/shard_map/split | solution.py:11
  15.6 63.3 %all_to_all.5 = bf16[32,64,1,512]{3,1,2,0:T(8,128)(2,1)S(1)} all-to-all(bf16[32,64,1,512]{3,1,2,0:T(8,128)(2,1)S(1)} %constant_dynamic-update-slice_fusion), channel_id=1, replica_groups=mesh['grp'=16,'aux'=32] {'aux'}, dimensions={0} | all-to-all | bytes 4194304 | tf_op jit(solution)/shard_map/all_to_all | solution.py:13
  78.9 1.0 fusion.10
  79.9 1.3 bitcast_convert_fusion
  81.2 0.3 copy.587
  81.5 0.2 bitcast_convert_fusion.2
  81.7 0.0 copy-start
  81.7 1.3 copy.586
  83.1 1.6 copy.588
  84.6 17.1 %all-gather.3.cloned.1.call-done = bf16[4,512,512]{2,1,0:T(8,128)(2,1)} async-done(((bf16[4,16,512]{2,1,0:T(8,128)(2,1)}), bf16[4,512,512]{2,1,0:T(8,128)(2,1)}) %all-gather.3.cloned.1.call-update) | async-done | bytes 2097168 | tf_op jit(solution)/shard_map/all_gather | solution.py:18
  101.7 0.0 copy-done
  101.7 1.5 convolution_convert_fusion
  103.2 85.1 %all-gather.5.cloned.1.call-done = bf16[6,512,512]{2,1,0:T(8,128)(2,1)} async-done(((bf16[6,16,512]{2,1,0:T(8,128)(2,1)}), bf16[6,512,512]{2,1,0:T(8,128)(2,1)}) %all-gather.5.cloned.1.call-update) | async-done | bytes 3145744 | tf_op jit(solution)/shard_map/all_gather | solution.py:19
  188.3 2.5 %fusion.4 = f32[512,512]{0,1:T(8,128)} fusion(f32[512,512]{0,1:T(8,128)S(1)} %copy.587, bf16[512,512]{0,1:T(8,128)(2,1)S(1)} %convolution_convert_fusion, bf16[6,512,512]{2,1,0:T(8,128)(2,1)} %all-gather.5.cloned.1.call-done), kind=kOutput, calls=%fused_computation.10 | convolution fusion | flops 268697600 | bytes 3145728 | tf_op jit(solution)/shard_map/dot_general | solution.py:33
  190.8 2.4 %convolution_convert_fusion.3 = bf16[512,512]{0,1:T(8,128)(2,1)S(1)} fusion(f32[512,512]{0,1:T(8,128)} %copy.586, bf16[512,512]{0,1:T(8,128)(2,1)S(1)} %convolution_convert_fusion, bf16[4,512,512]{2,1,0:T(8,128)(2,1)} %all-gather.3.cloned.1.call-done, bf16[6,512,512]{2,1,0:T(8,128)(2,1)} %all-gather.5.cloned.1.call-done), kind=kOutput, calls=%fused_computation.16 | convolution fusion | flops 537657344 | bytes 3145728 | tf_op jit(solution)/shard_map/dot_general | solution.py:38
  193.2 1.5 fusion.2
  194.7 3.2 %convolution_convert_fusion.2 = bf16[512,512]{0,1:T(8,128)(2,1)} fusion(f32[512,512]{0,1:T(8,128)} %fusion.4, bf16[512,512]{0,1:T(8,128)(2,1)S(1)} %convolution_convert_fusion.3, bf16[4,512,512]{2,1,0:T(8,128)(2,1)} %all-gather.3.cloned.1.call-done, bf16[6,512,512]{2,1,0:T(8,128)(2,1)} %all-gather.5.cloned.1.call-done), kind=kOutput, calls=%fused_computation.15 | convolution fusion | flops 537657344 | bytes 3145728 | tf_op jit(solution)/shard_map/dot_general | solution.py:38
  197.9 1.5 fusion.1
  199.4 0.0 copy-start.1
  199.5 2.3 %fusion.9 = bf16[512,512]{1,0:T(8,128)(2,1)S(1)} fusion(f32[512,512]{0,1:T(8,128)S(1)} %fusion.1, bf16[512,512]{0,1:T(8,128)(2,1)} %convolution_convert_fusion.2, bf16[4,512,512]{2,1,0:T(8,128)(2,1)} %all-gather.3.cloned.1.call-done, bf16[6,512,512]{2,1,0:T(8,128)(2,1)} %all-gather.5.cloned.1.call-done), kind=kOutput, calls=%fused_computation.20 | convolution fusion | flops 537657344 | bytes 3145728 | tf_op jit(solution)/shard_map/dot_general | solution.py:38
  201.7 0.0 copy-done.1
  201.7 1.5 pad_maximum_fusion
  (32 shorter events, 0.4 us)
Async XLA Ops:
  6.5 95.2 %all-gather.3.cloned.1.call-start = ((), (), s32[]{:S(2)}) async-start(), calls=%async_computation.1 | async-start | bytes 2162688 | tf_op jit(solution)/shard_map/all_gather | solution.py:18
  7.3 181.1 %all-gather.5.cloned.1.call-start = ((), (), s32[]{:S(2)}) async-start(), calls=%async_computation.2 | async-start | bytes 3244032 | tf_op jit(solution)/shard_map/all_gather | solution.py:19
  81.7 20.0 %copy-start = (bf16[8,64,1,512]{3,1,2,0:T(8,128)(2,1)S(1)}, bf16[8,64,1,512]{3,1,2,0:T(8,128)(2,1)}, u32[]{:S(2)}) copy-start(bf16[8,64,1,512]{3,1,2,0:T(8,128)(2,1)} %get-tuple-element.8) | copy-start | bytes 1572868
  199.4 2.3 %copy-start.1 = (bf16[512,512]{0,1:T(8,128)(2,1)S(1)}, bf16[512,512]{0,1:T(8,128)(2,1)}, u32[]{:S(2)}) copy-start(bf16[512,512]{0,1:T(8,128)(2,1)} %convolution_convert_fusion.2) | copy-start | bytes 1572868
Sparse Core Ops, SparseCore 0:
  10.5 91.1 all-gather.2
  104.9 83.3 all-gather.4
